TPU v7x, 32 devices: a whole 2x2x4 slice. The times are simulated.
32 devices in a mesh: dp: 16 (over z, y, core), mp: 2 (over x).
Axes of the slice: x: 2, y: 2, z: 4, core: 2. Of those that a mesh axis runs over, the one named last changes fastest.
Arguments:
- tokens: bfloat16 [8192, 768], P(('dp', 'mp')), may hold values from -6 to 6
- cotangent: bfloat16 [8192, 768], P(('dp', 'mp')), may hold values from -6 to 6
- lengths: int32 [32, 8], P(('dp', 'mp')), may hold values from 1 to 202, 256 in all within a row
- random_proj: float32 [2, 12, 64, 32], replicated, may hold values from -5 to 5
- attn_weight: bfloat16 [2, 3, 768, 768], P(None, None, None, 'mp'), may hold values from -0.21875 to 0.21875
- attn_bias: bfloat16 [2, 3, 768], P(None, None, 'mp'), may hold values from -1 to 1
- out_weight: bfloat16 [2, 768, 768], P(None, 'mp'), may hold values from -0.875 to 0.875
- norm_gains: bfloat16 [2, 2, 768], replicated, may hold values from 0.5 to 1.5
- biases: bfloat16 [2, 4, 768], replicated, may hold values from -1 to 1
- up_weight: bfloat16 [2, 768, 3072], P(None, None, 'mp'), may hold values from -0.21875 to 0.21875
- up_bias: bfloat16 [2, 3072], P(None, 'mp'), may hold values from -1 to 1
- down_weight: bfloat16 [2, 3072, 768], P(None, 'mp'), may hold values from -0.109375 to 0.109375
Outputs:
- stack_out: bfloat16 [8192, 768], P(('dp', 'mp'))
- tokens_grad: float32 [8192, 768], P(('dp', 'mp'))
- attn_weight_grad: float32 [2, 3, 768, 768], P(None, None, None, 'mp')
- attn_bias_grad: float32 [2, 3, 768], P(None, None, 'mp')
- out_weight_grad: float32 [2, 768, 768], P(None, 'mp')
- norm_gains_grad: float32 [2, 2, 768], P(None, None, 'mp')
- biases_grad: float32 [2, 4, 768], P(None, None, 'mp')
- up_weight_grad: float32 [2, 768, 3072], P(None, None, 'mp')
- up_bias_grad: float32 [2, 3072], P(None, 'mp')
- down_weight_grad: float32 [2, 3072, 768], P(None, 'mp')
Inputs may be any that keep to these rules, and one draw needn't show every extreme that they name: `lengths`: each row sums to 256 and its largest entry is 202.
All inputs are finite; a program needn't handle non-finite values.
Results may differ from a plain program's by a relative error of at most 0.012.
Values may be sent and summed in bfloat16 or wider, within the bound.
A program may use at most 256 MiB of HBM per device.

v0:
```python
import math

import jax
import jax.numpy as jnp
from jax import lax
from jax.sharding import PartitionSpec as P

highest = lax.Precision.HIGHEST


def layer_norm(values, scaling, shifting):
    average = jnp.mean(values, axis=-1, keepdims=True)
    centred = values - average
    spread = jnp.mean(centred * centred, axis=-1, keepdims=True)
    return centred * lax.rsqrt(spread + 1e-05) * scaling + shifting


def positions(lengths_row, row_count, head_size):
    finish = jnp.cumsum(lengths_row, dtype=jnp.int32)
    counter = jnp.arange(row_count, dtype=jnp.int32)
    passed = counter[:, None] >= finish[None, :]
    segment = jnp.sum(passed.astype(jnp.int32), axis=1, dtype=jnp.int32)
    start_at = jnp.sum(jnp.where(passed, lengths_row[None, :], 0), axis=1, dtype=jnp.int32)
    offset = (counter - start_at).astype(jnp.float32)
    half_size = head_size // 2
    frequency = jnp.exp(
        jnp.arange(half_size, dtype=jnp.float32) * (-2.0 * math.log(10000.0) / head_size)
    )
    angles = offset[:, None] * frequency[None, :]
    same_mol = (segment[:, None] == segment[None, :]).astype(jnp.float32)
    return (jnp.cos(angles)[:, None, :], jnp.sin(angles)[:, None, :], same_mol)


def rotate(vectors, cosines, sines):
    half_size = vectors.shape[-1] // 2
    leading = vectors[..., :half_size]
    trailing = vectors[..., half_size:]
    return jnp.concatenate(
        [leading * cosines - trailing * sines, trailing * cosines + leading * sines], axis=-1
    )


def features(vectors, random_proj):
    scaled = vectors * vectors.shape[-1] ** (-0.25)
    return jax.nn.softplus(jnp.einsum("thd,hdm->thm", scaled, random_proj, precision=highest))


def attend(queries, key_rows, values, random_proj, cosines, sines, same_mol):
    row_count, model_width = queries.shape
    head_count, head_size = (random_proj.shape[0], random_proj.shape[1])
    shaped = (row_count, head_count, head_size)
    query_feats = features(rotate(queries.reshape(shaped), cosines, sines), random_proj)
    key_feats = features(rotate(key_rows.reshape(shaped), cosines, sines), random_proj)
    scores = jnp.einsum("thm,shm->hts", query_feats, key_feats, precision=highest) * same_mol[None]
    numerator = jnp.einsum("hts,shd->thd", scores, values.reshape(shaped), precision=highest)
    denominator = jnp.sum(scores, axis=2).T[:, :, None]
    return (numerator / denominator).reshape(row_count, model_width)


def gelu_exact(values):
    return jax.nn.gelu(values, approximate=False)


def on_device(
    tokens,
    cotangent,
    lengths,
    random_proj,
    attn_weight,
    attn_bias,
    out_weight,
    norm_gains,
    biases,
    up_weight,
    up_bias,
    down_weight,
):
    layer_count = attn_weight.shape[0]
    head_size = random_proj.shape[2]
    local_heads = attn_weight.shape[3] // head_size
    head_start = lax.axis_index("mp") * local_heads
    gain_values = norm_gains.astype(jnp.float32)
    shift_values = biases.astype(jnp.float32)
    current = tokens.astype(jnp.float32)
    kept_values = []
    for layer_index in range(layer_count):
        normed = layer_norm(
            current, gain_values[layer_index, 0], shift_values[layer_index, 0]
        ).astype(jnp.bfloat16)
        full_attn, full_bias, full_out = (
            attn_weight[layer_index],
            attn_bias[layer_index],
            out_weight[layer_index],
        )
        attn_inputs, group_lengths = (
            lax.all_gather(normed, "mp", axis=0, tiled=True),
            lax.all_gather(lengths, "mp", axis=0, tiled=True),
        )
        layer_proj = lax.dynamic_slice_in_dim(random_proj[layer_index], head_start, local_heads, 0)
        place_info = positions(group_lengths.reshape(-1), attn_inputs.shape[0], head_size)
        projected = (
            jnp.einsum("td,jde->jte", attn_inputs, full_attn, preferred_element_type=jnp.float32)
            + full_bias.astype(jnp.float32)[:, None, :]
        )
        context = attend(
            projected[0],
            projected[1],
            projected[2],
            layer_proj,
            place_info[0],
            place_info[1],
            place_info[2],
        ).astype(jnp.bfloat16)
        attn_branch = lax.psum_scatter(
            jnp.dot(context, full_out, preferred_element_type=jnp.float32).astype(jnp.bfloat16),
            "mp",
            scatter_dimension=0,
            tiled=True,
        ).astype(jnp.float32)
        middle = current + attn_branch + shift_values[layer_index, 1]
        second = layer_norm(
            middle, gain_values[layer_index, 1], shift_values[layer_index, 2]
        ).astype(jnp.bfloat16)
        up_full, up_shift, down_full = (
            up_weight[layer_index],
            up_bias[layer_index],
            down_weight[layer_index],
        )
        row_inputs = lax.all_gather(second, "mp", axis=0, tiled=True)
        hidden = jnp.dot(row_inputs, up_full, preferred_element_type=jnp.float32) + up_shift.astype(
            jnp.float32
        )
        active = gelu_exact(hidden).astype(jnp.bfloat16)
        branch = lax.psum_scatter(
            jnp.dot(active, down_full, preferred_element_type=jnp.float32).astype(jnp.bfloat16),
            "mp",
            scatter_dimension=0,
            tiled=True,
        ).astype(jnp.float32)
        kept_values.append(
            (
                current,
                attn_inputs,
                projected,
                context,
                middle,
                row_inputs,
                hidden,
                active,
                full_attn,
                full_out,
                up_full,
                down_full,
                layer_proj,
                place_info,
            )
        )
        current = middle + branch + shift_values[layer_index, 3]
    stack_out = current.astype(jnp.bfloat16)
    grad_now = cotangent.astype(jnp.float32)
    layer_grads = [None] * layer_count
    for layer_index in reversed(range(layer_count)):
        (
            layer_in,
            attn_inputs,
            projected,
            context,
            middle,
            row_inputs,
            hidden,
            active,
            full_attn,
            full_out,
            up_full,
            down_full,
            layer_proj,
            place_info,
        ) = kept_values[layer_index]
        branch_grad = grad_now.astype(jnp.bfloat16)
        rows_grad = lax.all_gather(branch_grad, "mp", axis=0, tiled=True)
        down_grad = jnp.dot(active.T, rows_grad, preferred_element_type=jnp.float32)
        active_grad = jnp.dot(rows_grad, down_full.T, preferred_element_type=jnp.float32)
        gelu_pull = jax.vjp(gelu_exact, hidden)[1]
        hidden_grad = gelu_pull(active_grad)[0].astype(jnp.bfloat16)
        up_grad = jnp.dot(row_inputs.T, hidden_grad, preferred_element_type=jnp.float32)
        up_shift_grad = jnp.sum(hidden_grad.astype(jnp.float32), axis=0)
        second_grad = lax.psum_scatter(
            jnp.dot(hidden_grad, up_full.T, preferred_element_type=jnp.float32).astype(
                jnp.bfloat16
            ),
            "mp",
            scatter_dimension=0,
            tiled=True,
        ).astype(jnp.float32)
        second_pull = jax.vjp(
            layer_norm, middle, gain_values[layer_index, 1], shift_values[layer_index, 2]
        )[1]
        middle_grad, gain_two, shift_two = second_pull(second_grad)
        middle_grad = middle_grad + grad_now
        attn_grad = middle_grad.astype(jnp.bfloat16)
        attn_grad_rows = lax.all_gather(attn_grad, "mp", axis=0, tiled=True)
        out_grad = jnp.dot(context.T, attn_grad_rows, preferred_element_type=jnp.float32)
        context_grad = jnp.dot(attn_grad_rows, full_out.T, preferred_element_type=jnp.float32)

        def attend_local(queries, key_rows, values):
            return attend(
                queries, key_rows, values, layer_proj, place_info[0], place_info[1], place_info[2]
            )

        attend_pull = jax.vjp(attend_local, projected[0], projected[1], projected[2])[1]
        triple_grad = jnp.stack(attend_pull(context_grad)).astype(jnp.bfloat16)
        attn_weight_grad = jnp.einsum(
            "td,jte->jde", attn_inputs, triple_grad, preferred_element_type=jnp.float32
        )
        attn_bias_grad = jnp.sum(triple_grad.astype(jnp.float32), axis=1)
        normed_grad = lax.psum_scatter(
            jnp.einsum(
                "jte,jde->td", triple_grad, full_attn, preferred_element_type=jnp.float32
            ).astype(jnp.bfloat16),
            "mp",
            scatter_dimension=0,
            tiled=True,
        ).astype(jnp.float32)
        first_pull = jax.vjp(
            layer_norm, layer_in, gain_values[layer_index, 0], shift_values[layer_index, 0]
        )[1]
        input_grad, gain_one, shift_one = first_pull(normed_grad)
        small_grads = jnp.stack(
            [
                gain_one,
                gain_two,
                shift_one,
                jnp.sum(attn_grad.astype(jnp.float32), axis=0),
                shift_two,
                jnp.sum(branch_grad.astype(jnp.float32), axis=0),
            ]
        )
        grad_now = input_grad + middle_grad
        small_part = lax.psum_scatter(small_grads, "mp", scatter_dimension=1, tiled=True)
        attn_shares = (attn_weight_grad, attn_bias_grad, out_grad, small_part)
        ffn_part = (up_grad, up_shift_grad, down_grad)
        shares = attn_shares + ffn_part
        shares = tuple(
            lax.psum(
                (shares[0], shares[1], shares[2], shares[3], shares[4], shares[5], shares[6]), "dp"
            )
        )
        layer_grads[layer_index] = shares
    stacked = tuple(
        (
            jnp.stack([layer_grads[layer_index][member] for layer_index in range(layer_count)])
            for member in range(7)
        )
    )
    return (
        stack_out,
        grad_now,
        stacked[0],
        stacked[1],
        stacked[2],
        stacked[3][:, :2],
        stacked[3][:, 2:],
        stacked[4],
        stacked[5],
        stacked[6],
    )


def solution(mesh):
    return jax.shard_map(
        on_device,
        mesh=mesh,
        in_specs=(
            P(("dp", "mp"), None),
            P(("dp", "mp"), None),
            P(("dp", "mp"), None),
            P(),
            P(None, None, None, "mp"),
            P(None, None, "mp"),
            P(None, "mp", None),
            P(),
            P(),
            P(None, None, "mp"),
            P(None, "mp"),
            P(None, "mp", None),
        ),
        out_specs=(
            P(("dp", "mp"), None),
            P(("dp", "mp"), None),
            P(None, None, None, "mp"),
            P(None, None, "mp"),
            P(None, "mp", None),
            P(None, None, "mp"),
            P(None, None, "mp"),
            P(None, None, "mp"),
            P(None, "mp"),
            P(None, "mp", None),
        ),
        check_vma=False,
    )
```

profile of v0, /device:TPU:0, one launch (start us, length us, event | category | flops | bytes accessed | tf_op | source)
XLA Modules:
  0.0 1000.4 jit_solution(13332367531663909116)
XLA Ops:
  7.3 5.4 all-gather
  21.5 10.7 %all_gather.28 = bf16[512,768]{1,0:T(8,128)(2,1)S(1)} all-gather(bf16[256,768]{1,0:T(8,128)(2,1)S(1)} %fusion.135), channel_id=1, replica_groups=mesh['dp'=16,'mp'=2] {'mp'}, dimensions={0}, use_global_device_ids=true | all-gather | bytes 1179648 | tf_op jit(solution)/shard_map/all_gather | solution.py:96
  36.8 5.3 multiply_reduce_fusion.1
  42.2 5.2 divide_convert_fusion.1
  49.6 18.4 %reduce-scatter.11.cloned.1.call-done = bf16[256,768]{1,0:T(8,128)(2,1)} async-done(((bf16[512,768]{1,0:T(8,128)(2,1)}), bf16[256,768]{1,0:T(8,128)(2,1)}) %reduce-scatter.11.cloned.1.call-update) | async-done | bytes 393232 | tf_op jit(solution)/shard_map/reduce_scatter | solution.py:114
  71.9 11.5 %all_gather.30 = bf16[512,768]{1,0:T(8,128)(2,1)S(1)} all-gather(bf16[256,768]{1,0:T(8,128)(2,1)S(1)} %add_convert_fusion.9), channel_id=1, replica_groups=mesh['dp'=16,'mp'=2] {'mp'}, dimensions={0}, use_global_device_ids=true | all-gather | bytes 1179648 | tf_op jit(solution)/shard_map/all_gather | solution.py:129
  83.4 11.0 %multiply_convert_fusion.1 = (bf16[512,1536]{1,0:T(8,128)(2,1)S(1)}, f32[512,1536]{1,0:T(8,128)}, f32[512,1536]{1,0:T(8,128)}) fusion(f32[1536]{0:T(1024)S(1)} %get-tuple-element.94, bf16[512,768]{1,0:T(8,128)(2,1)S(1)} %all_gather.30, bf16[2,768,1536]{2,1,0:T(8,128)(2,1)} %param.22), kind=kOutput, calls=%fused_computation.50 | convolution fusion | flops 1259864064 | bytes 11016192 | tf_op jit(solution)/shard_map/dot_general | solution.py:130
  98.0 17.5 %reduce-scatter.13.cloned.1.call-done = bf16[256,768]{1,0:T(8,128)(2,1)} async-done(((bf16[512,768]{1,0:T(8,128)(2,1)}), bf16[256,768]{1,0:T(8,128)(2,1)}) %reduce-scatter.13.cloned.1.call-update) | async-done | bytes 393232 | tf_op jit(solution)/shard_map/reduce_scatter | solution.py:134
  117.4 12.0 %all_gather.31 = bf16[512,768]{1,0:T(8,128)(2,1)S(1)} all-gather(bf16[256,768]{1,0:T(8,128)(2,1)S(1)} %add_convert_fusion.8), channel_id=1, replica_groups=mesh['dp'=16,'mp'=2] {'mp'}, dimensions={0}, use_global_device_ids=true | all-gather | bytes 1179648 | tf_op jit(solution)/shard_map/all_gather | solution.py:96
  133.6 5.3 multiply_reduce_fusion
  138.9 5.0 divide_convert_fusion
  145.7 15.4 %all_gather.33 = bf16[512,768]{1,0:T(8,128)(2,1)} all-gather(bf16[256,768]{1,0:T(8,128)(2,1)S(1)} %copy-done.23), channel_id=1, replica_groups=mesh['dp'=16,'mp'=2] {'mp'}, dimensions={0}, use_global_device_ids=true | all-gather | bytes 1179648 | tf_op jit(solution)/shard_map/all_gather | solution.py:180
  161.1 4.8 reduce-scatter.15.cloned.1.call-done
  169.4 11.8 %all_gather.32 = bf16[512,768]{1,0:T(8,128)(2,1)S(1)} all-gather(bf16[256,768]{1,0:T(8,128)(2,1)S(1)} %add_convert_fusion.7), channel_id=1, replica_groups=mesh['dp'=16,'mp'=2] {'mp'}, dimensions={0}, use_global_device_ids=true | all-gather | bytes 1179648 | tf_op jit(solution)/shard_map/all_gather | solution.py:129
  181.2 10.3 %multiply_convert_fusion = (bf16[512,1536]{1,0:T(8,128)(2,1)}, f32[512,1536]{1,0:T(8,128)S(1)}, f32[512,1536]{1,0:T(8,128)S(1)}) fusion(f32[1536]{0:T(1024)S(1)} %copy-done.116, bf16[512,768]{1,0:T(8,128)(2,1)S(1)} %all_gather.32, bf16[2,768,1536]{2,1,0:T(8,128)(2,1)} %param.22), kind=kOutput, calls=%fused_computation.37 | convolution fusion | flops 1259864064 | bytes 11016192 | tf_op jit(solution)/shard_map/dot_general | solution.py:130
  191.5 3.1 convert_reduce_fusion
  198.1 4.4 fusion.87
  206.3 9.3 reduce-scatter.19.cloned.1.call-done
  218.8 16.4 %reduce-scatter.17.cloned.1.call-done = bf16[256,768]{1,0:T(8,128)(2,1)} async-done(((bf16[512,768]{1,0:T(8,128)(2,1)}), bf16[256,768]{1,0:T(8,128)(2,1)}) %reduce-scatter.17.cloned.1.call-update) | async-done | bytes 393232 | tf_op jit(solution)/shard_map/reduce_scatter | solution.py:134
  239.6 12.0 %all_gather.34 = bf16[512,768]{1,0:T(8,128)(2,1)S(1)} all-gather(bf16[256,768]{1,0:T(8,128)(2,1)S(1)} %get-tuple-element.112), channel_id=1, replica_groups=mesh['dp'=16,'mp'=2] {'mp'}, dimensions={0}, use_global_device_ids=true | all-gather | bytes 1179648 | tf_op jit(solution)/shard_map/all_gather | solution.py:201
  253.0 8.7 fusion.107
  261.8 5.2 fusion.180
  267.0 7.4 fusion.121
  274.5 5.4 fusion.118
  289.4 3.9 bitcast_convert_fusion.1
  293.5 17.6 %reduce-scatter.21.cloned.1.call-done = bf16[256,768]{1,0:T(8,128)(2,1)} async-done(((bf16[512,768]{1,0:T(8,128)(2,1)}), bf16[256,768]{1,0:T(8,128)(2,1)}) %reduce-scatter.21.cloned.1.call-update) | async-done | bytes 393232 | tf_op jit(solution)/shard_map/reduce_scatter | solution.py:216
  317.8 11.5 %all_gather.35 = bf16[512,768]{1,0:T(8,128)(2,1)S(1)} all-gather(bf16[256,768]{1,0:T(8,128)(2,1)S(1)} %get-tuple-element.114), channel_id=1, replica_groups=mesh['dp'=16,'mp'=2] {'mp'}, dimensions={0}, use_global_device_ids=true | all-gather | bytes 1179648 | tf_op jit(solution)/shard_map/all_gather | solution.py:180
  329.4 4.9 convert_reduce_fusion.1
  338.5 16.9 %reduce-scatter.23.cloned.1.call-done = bf16[256,768]{1,0:T(8,128)(2,1)} async-done(((bf16[512,768]{1,0:T(8,128)(2,1)}), bf16[256,768]{1,0:T(8,128)(2,1)}) %reduce-scatter.23.cloned.1.call-update) | async-done | bytes 393232 | tf_op jit(solution)/shard_map/reduce_scatter | solution.py:187
  361.5 11.9 %all_gather.36 = bf16[512,768]{1,0:T(8,128)(2,1)S(1)} all-gather(bf16[256,768]{1,0:T(8,128)(2,1)S(1)} %get-tuple-element.117), channel_id=1, replica_groups=mesh['dp'=16,'mp'=2] {'mp'}, dimensions={0}, use_global_device_ids=true | all-gather | bytes 1179648 | tf_op jit(solution)/shard_map/all_gather | solution.py:201
  375.3 9.5 fusion.104
  384.8 5.2 fusion.181
  390.0 7.4 fusion.115
  397.4 5.4 fusion.112
  415.5 3.7 bitcast_convert_fusion
  419.5 5.4 convolution_bitcast_fusion
  424.9 3.6 convolution_bitcast_fusion.2
  430.2 3.0 convolution_bitcast_fusion.4
  433.9 5.2 convolution_bitcast_fusion.3
  439.0 3.6 convolution_bitcast_fusion.1
  442.8 4.4 convolution_bitcast_fusion.5
  457.7 6.7 reduce-scatter.27.cloned.1.call-done
  464.4 64.7 %all-reduce.8 = (f32[1,3,384]{2,1,0:T(4,128)S(1)}, f32[1,3,384]{2,1,0:T(4,128)S(1)}, f32[1,6,384]{2,1,0:T(8,128)S(1)}, f32[1,6,384]{2,1,0:T(8,128)S(1)}, f32[1,1536]{1,0:T(1,128)S(1)}, /*index=5*/f32[1,1536]{1,0:T(1,128)S(1)}) all-reduce(f32[1,3,384]{2,1,0:T(4,128)S(1)} %bitcast.296, ...), channel_id=1, replica_groups=mesh['dp'=16,'mp'=2] {'dp'}, use_global_device_ids=true, to_apply=%region_38.40 | all-reduce | flops 9984 | bytes 79872 | tf_op jit(solution)/shard_map/psum | solution.py:244
  531.6 432.0 %all-reduce.12.cloned.1.call-done = (f32[1,3,768,384]{2,3,1,0:T(8,128)}, f32[1,3,768,384]{2,3,1,0:T(8,128)}, f32[1,384,768]{2,1,0:T(8,128)}, f32[1,384,768]{2,1,...) async-done(((f32[1,3,768,384]{2,3,1,0:T(8,128)}, f32[1,3,768,384]{2,3,1,0:T(8,128)}, ...) | async-done | bytes 28311568 | tf_op jit(solution)/shard_map/psum | solution.py:244
  963.6 6.9 pad_maximum_fusion.2
  970.5 8.2 copy.119
  980.3 8.8 pad_maximum_fusion
  989.1 4.3 pad_maximum_fusion.1
  (429 shorter events, 108.4 us)
Async XLA Ops:
  7.2 25.0 %copy-start.61 = (f32[2,12,64,32]{2,3,1,0:T(8,128)S(1)}, f32[2,12,64,32]{2,3,1,0:T(8,128)}, u32[]{:S(2)}) copy-start(f32[2,12,64,32]{2,3,1,0:T(8,128)} %param.16) | copy-start | bytes 589828
  7.2 60.7 %reduce-scatter.11.cloned.1.call-start = ((), (), s32[]{:S(2)}) async-start(), calls=%async_computation.10 | async-start | bytes 1179648 | tf_op jit(solution)/shard_map/reduce_scatter | solution.py:114
  15.1 17.9 %copy-start.76 = (f32[256]{0:T(256)}, f32[256]{0:T(256)S(1)}, u32[]{:S(2)}) copy-start(f32[256]{0:T(256)S(1)} %broadcast_multiply_fusion.3) | copy-start | bytes 3076
  16.4 16.7 %copy-start.88 = (f32[256]{0:T(256)}, f32[256]{0:T(256)S(1)}, u32[]{:S(2)}) copy-start(f32[256]{0:T(256)S(1)} %fusion.207) | copy-start | bytes 3076
  16.6 16.6 %copy-start.119 = (bf16[2,3,768,384]{3,2,1,0:T(8,128)(2,1)S(1)}, bf16[2,3,768,384]{3,2,1,0:T(8,128)(2,1)}, u32[]{:S(2)}) copy-start(bf16[2,3,768,384]{3,2,1,0:T(8,128)(2,1)} %param.17) | copy-start | bytes 10616836
  42.2 25.7 %copy-start = (bf16[256,768]{1,0:T(8,128)(2,1)S(1)}, bf16[256,768]{1,0:T(8,128)(2,1)}, u32[]{:S(2)}) copy-start(bf16[256,768]{1,0:T(8,128)(2,1)} %param.13) | copy-start | bytes 1179652
  42.2 25.7 %copy-start.62 = (f32[768]{0:T(1024)S(1)}, f32[768]{0:T(1024)}, u32[]{:S(2)}) copy-start(f32[768]{0:T(1024)} %get-tuple-element.87) | copy-start | bytes 9220
  47.4 36.0 %copy-start.31 = (bf16[512,6,64]{0,2,1:T(8,128)(2,1)}, bf16[512,6,64]{0,2,1:T(8,128)(2,1)S(1)}, u32[]{:S(2)}) copy-start(bf16[512,6,64]{0,2,1:T(8,128)(2,1)S(1)} %get-tuple-element.170) | copy-start | bytes 1179652
  47.4 23.1 %copy-start.66 = (f32[768]{0:T(1024)S(1)}, f32[768]{0:T(1024)}, u32[]{:S(2)}) copy-start(f32[768]{0:T(1024)} %get-tuple-element.187) | copy-start | bytes 9220
  47.4 23.1 %copy-start.100 = (f32[768]{0:T(1024)S(1)}, f32[768]{0:T(1024)}, u32[]{:S(2)}) copy-start(f32[768]{0:T(1024)} %get-tuple-element.86) | copy-start | bytes 9220
  48.9 66.6 %reduce-scatter.13.cloned.1.call-start = ((), (), s32[]{:S(2)}) async-start(), calls=%async_computation.11 | async-start | bytes 1179648 | tf_op jit(solution)/shard_map/reduce_scatter | solution.py:134
  69.1 25.3 %copy-start.73 = (f32[256]{0:T(256)}, f32[256]{0:T(256)S(1)}, u32[]{:S(2)}) copy-start(f32[256]{0:T(256)S(1)} %broadcast_multiply_fusion.2) | copy-start | bytes 3076
  70.4 24.0 %copy-start.110 = (f32[256]{0:T(256)}, f32[256]{0:T(256)S(1)}, u32[]{:S(2)}) copy-start(f32[256]{0:T(256)S(1)} %multiply_reduce_fusion.6) | copy-start | bytes 3076
  70.4 24.0 %copy-start.80 = (f32[256]{0:T(256)}, f32[256]{0:T(256)S(1)}, u32[]{:S(2)}) copy-start(f32[256]{0:T(256)S(1)} %fusion.208) | copy-start | bytes 3076
  70.5 25.1 %slice-start.4 = ((s8[4718592]{0:T(1024)(128)(4,1)}), s8[4194304]{0:T(1024)(128)(4,1)S(1)}, s32[]{:S(2)}) async-start(s8[4718592]{0:T(1024)(128)(4,1)} %bitcast.303), calls=%async_computation.25 | async-start | bytes 8388608
  95.6 19.9 %copy-start.3 = (bf16[256,768]{1,0:T(8,128)(2,1)S(1)}, bf16[256,768]{1,0:T(8,128)(2,1)}, u32[]{:S(2)}) copy-start(bf16[256,768]{1,0:T(8,128)(2,1)} %reduce-scatter.11.cloned.1.call-done) | copy-start | bytes 1179652
  95.6 19.9 %copy-start.63 = (f32[768]{0:T(1024)S(1)}, f32[768]{0:T(1024)}, u32[]{:S(2)}) copy-start(f32[768]{0:T(1024)} %get-tuple-element.87) | copy-start | bytes 9220
  95.6 19.9 %copy-start.99 = (f32[768]{0:T(1024)S(1)}, f32[768]{0:T(1024)}, u32[]{:S(2)}) copy-start(f32[768]{0:T(1024)} %get-tuple-element.85) | copy-start | bytes 9220
  97.9 19.3 %copy-start.71 = (f32[768]{0:T(1024)S(1)}, f32[768]{0:T(1024)}, u32[]{:S(2)}) copy-start(f32[768]{0:T(1024)} %get-tuple-element.188) | copy-start | bytes 9220
  97.9 19.4 %copy-start.98 = (f32[768]{0:T(1024)S(1)}, f32[768]{0:T(1024)}, u32[]{:S(2)}) copy-start(f32[768]{0:T(1024)} %get-tuple-element.84) | copy-start | bytes 9220
  97.9 68.0 %reduce-scatter.15.cloned.1.call-start = ((), (), s32[]{:S(2)}) async-start(), calls=%async_computation.12 | async-start | bytes 1179648 | tf_op jit(solution)/shard_map/reduce_scatter | solution.py:114
  143.9 22.0 %copy-start.33 = (bf16[512,6,64]{0,2,1:T(8,128)(2,1)}, bf16[512,6,64]{0,2,1:T(8,128)(2,1)S(1)}, u32[]{:S(2)}) copy-start(bf16[512,6,64]{0,2,1:T(8,128)(2,1)S(1)} %get-tuple-element.175) | copy-start | bytes 1179652
  145.6 70.0 %reduce-scatter.19.cloned.1.call-start = ((), (), s32[]{:S(2)}) async-start(), calls=%async_computation.14 | async-start | bytes 1179648 | tf_op jit(solution)/shard_map/reduce_scatter | solution.py:187
  165.9 25.6 %slice-start.6 = ((s8[4718592]{0:T(1024)(128)(4,1)}), s8[4194304]{0:T(1024)(128)(4,1)S(1)}, s32[]{:S(2)}) async-start(s8[4718592]{0:T(1024)(128)(4,1)} %bitcast.305), calls=%async_computation.27 | async-start | bytes 8388608
  165.9 29.9 %slice-start.8 = ((s8[4718592]{0:T(1024)(128)(4,1)}), s8[4194304]{0:T(1024)(128)(4,1)S(1)}, s32[]{:S(2)}) async-start(s8[4718592]{0:T(1024)(128)(4,1)} %bitcast.307), calls=%async_computation.29 | async-start | bytes 8388608
  198.1 37.1 %reduce-scatter.17.cloned.1.call-start = ((), (), s32[]{:S(2)}) async-start(), calls=%async_computation.13 | async-start | bytes 1179648 | tf_op jit(solution)/shard_map/reduce_scatter | solution.py:134
  202.6 108.4 %reduce-scatter.21.cloned.1.call-start = ((), (), s32[]{:S(2)}) async-start(), calls=%async_computation.15 | async-start | bytes 1179648 | tf_op jit(solution)/shard_map/reduce_scatter | solution.py:216
  235.2 17.3 %copy-start.20 = (f32[512,6,64]{0,2,1:T(8,128)S(1)}, f32[512,6,64]{0,2,1:T(8,128)}, u32[]{:S(2)}) copy-start(f32[512,6,64]{0,2,1:T(8,128)} %get-tuple-element.176) | copy-start | bytes 2359300
  235.2 17.3 %copy-start.21 = (bf16[1,384,768]{2,1,0:T(8,128)(2,1)S(1)}, bf16[1,384,768]{2,1,0:T(8,128)(2,1)}, u32[]{:S(2)}) copy-start(bf16[1,384,768]{2,1,0:T(8,128)(2,1)} %get-tuple-element.134) | copy-start | bytes 1769476
  235.2 17.3 %copy-start.59 = (f32[512,6]{0,1:T(8,128)S(1)}, f32[512,6]{0,1:T(8,128)}, u32[]{:S(2)}) copy-start(f32[512,6]{0,1:T(8,128)} %divide_bitcast_fusion.1) | copy-start | bytes 36868
  289.4 21.6 %copy-start.72 = (f32[768]{0:T(1024)S(1)}, f32[768]{0:T(1024)}, u32[]{:S(2)}) copy-start(f32[768]{0:T(1024)} %get-tuple-element.188) | copy-start | bytes 9220
  289.4 21.6 %copy-start.79 = (f32[256]{0:T(256)S(1)}, f32[256]{0:T(256)}, u32[]{:S(2)}) copy-start(f32[256]{0:T(256)} %copy-done.78) | copy-start | bytes 3076
  289.4 23.6 %copy-start.113 = (f32[256]{0:T(256)S(1)}, f32[256]{0:T(256)}, u32[]{:S(2)}) copy-start(f32[256]{0:T(256)} %copy-done.112) | copy-start | bytes 3076
  289.4 23.6 %copy-start.105 = (f32[256]{0:T(256)S(1)}, f32[256]{0:T(256)}, u32[]{:S(2)}) copy-start(f32[256]{0:T(256)} %copy-done.104) | copy-start | bytes 3076
  293.4 62.0 %reduce-scatter.23.cloned.1.call-start = ((), (), s32[]{:S(2)}) async-start(), calls=%async_computation.16 | async-start | bytes 1179648 | tf_op jit(solution)/shard_map/reduce_scatter | solution.py:187
  311.0 18.4 %copy-start.124 = (f32[512,1536]{1,0:T(8,128)S(1)}, f32[512,1536]{1,0:T(8,128)}, u32[]{:S(2)}) copy-start(f32[512,1536]{1,0:T(8,128)} %get-tuple-element.172) | copy-start | bytes 9437188
  313.0 16.3 %copy-start.123 = (f32[512,1536]{1,0:T(8,128)S(1)}, f32[512,1536]{1,0:T(8,128)}, u32[]{:S(2)}) copy-start(f32[512,1536]{1,0:T(8,128)} %get-tuple-element.127) | copy-start | bytes 9437188
  315.3 20.2 %slice-start.10 = ((s8[4718592]{0:T(1024)(128)(4,1)}), s8[4194304]{0:T(1024)(128)(4,1)S(1)}, s32[]{:S(2)}) async-start(s8[4718592]{0:T(1024)(128)(4,1)} %bitcast.309), calls=%async_computation.31 | async-start | bytes 8388608
  335.4 20.0 %copy-start.64 = (f32[768]{0:T(1024)S(1)}, f32[768]{0:T(1024)}, u32[]{:S(2)}) copy-start(f32[768]{0:T(1024)} %get-tuple-element.87) | copy-start | bytes 9220
  335.4 20.0 %copy-start.67 = (f32[768]{0:T(1024)S(1)}, f32[768]{0:T(1024)}, u32[]{:S(2)}) copy-start(f32[768]{0:T(1024)} %get-tuple-element.187) | copy-start | bytes 9220
  335.5 19.9 %copy-start.74 = (f32[256]{0:T(256)S(1)}, f32[256]{0:T(256)}, u32[]{:S(2)}) copy-start(f32[256]{0:T(256)} %copy-done.73) | copy-start | bytes 3076
  335.5 21.9 %copy-start.111 = (f32[256]{0:T(256)S(1)}, f32[256]{0:T(256)}, u32[]{:S(2)}) copy-start(f32[256]{0:T(256)} %copy-done.110) | copy-start | bytes 3076
  335.5 21.9 %copy-start.81 = (f32[256]{0:T(256)S(1)}, f32[256]{0:T(256)}, u32[]{:S(2)}) copy-start(f32[256]{0:T(256)} %copy-done.80) | copy-start | bytes 3076
  337.8 109.5 %reduce-scatter.25.cloned.1.call-start = ((), (), s32[]{:S(2)}) async-start(), calls=%async_computation.17 | async-start | bytes 1179648 | tf_op jit(solution)/shard_map/reduce_scatter | solution.py:216
  355.4 18.1 %copy-start.60 = (f32[512,6]{0,1:T(8,128)S(1)}, f32[512,6]{0,1:T(8,128)}, u32[]{:S(2)}) copy-start(f32[512,6]{0,1:T(8,128)} %divide_bitcast_fusion) | copy-start | bytes 36868
  419.2 38.5 %reduce-scatter.29.cloned.1.call-start = ((), (), s32[]{:S(2)}) async-start(), calls=%async_computation.19 | async-start | bytes 36864 | tf_op jit(solution)/shard_map/reduce_scatter | solution.py:239
  442.7 21.7 %reduce-scatter.27.cloned.1.call-start = ((), (), s32[]{:S(2)}) async-start(), calls=%async_computation.18 | async-start | bytes 36864 | tf_op jit(solution)/shard_map/reduce_scatter | solution.py:239
  450.8 512.8 %all-reduce.12.cloned.1.call-start = ((), (), s32[]{:S(2)}) async-start(), calls=%async_computation.20 | async-start | bytes 56623104 | tf_op jit(solution)/shard_map/psum | solution.py:244
  (100 other events, 607.9 us)
Sparse Core Ops, SparseCore 0:
  49.0 18.8 reduce-scatter.10
  98.0 17.4 reduce-scatter.12
  145.8 20.0 reduce-scatter.14
  198.2 17.3 reduce-scatter.18
  217.7 17.4 reduce-scatter.16
  293.5 17.4 reduce-scatter.20
  337.9 17.4 reduce-scatter.22
  419.3 17.4 reduce-scatter.24
  442.7 9.7 reduce-scatter.28
  454.6 9.8 reduce-scatter.26
  471.3 492.3 all-reduce.11
where the time goes:
time: 1010 us; the launch traced here: 1000 us
  waiting for transfers between devices  540 us (53%)
  matrix products  168 us (17%)
  blocking collectives  167 us (17%)
  other arithmetic  74.8 us (7%)
  local copies, waits for them, and re-layouts  33.8 us (3%)
  between operations  16 us (2%)
    psum x1, waiting for transfers between devices, on_device(): lax.psum((shares[0], shares[1], shares[2], shares[3], shares[4], shares[5...  432 us
    psum x1, blocking collectives, on_device(): lax.psum((shares[0], shares[1], shares[2], shares[3], shares[4], shares[5...  64.7 us
    dot_general x6, matrix products, attend(): jnp.einsum('hts,shd->thd', scores, values.reshape(shaped), precision=high...  38.8 us
    dot_general x6, matrix products, attend(): jnp.einsum('thm,shm->hts', query_feats, key_feats, precision=highest)  36 us
    reduce_scatter x2, waiting for transfers between devices, on_device(): lax.psum_scatter(jnp.dot(active, down_full, preferred_element_type=jnp.fl...  33.9 us
    all_gather x2, blocking collectives, on_device(): rows_grad = lax.all_gather(branch_grad, 'mp', axis=0, tiled=True)  26.9 us
    reduce_scatter x2, waiting for transfers between devices, on_device(): lax.psum_scatter(jnp.dot(hidden_grad, up_full.T, preferred_element_type=j...  26.2 us
    all_gather x2, blocking collectives, on_device(): attn_grad_rows = lax.all_gather(attn_grad, 'mp', axis=0, tiled=True)  24 us
  transfers between devices with their start and end apart: 11, of which 9 were waited for; matrix products, arithmetic and copies ran while one was open for 5% of the time, Pallas kernels for 0%

commit v1 on v0

v1 whole, which is shorter than its diff:
```python
import functools
import math

import jax
import jax.numpy as jnp
from jax import lax
from jax.experimental import pallas as pl
from jax.experimental.pallas import tpu as pltpu
from jax.sharding import PartitionSpec as P

MESH = pl.DeviceIdType.MESH
W = 384


def rdma(src, dst, send, recv, dev):
    return pltpu.make_async_remote_copy(
        src_ref=src, dst_ref=dst, send_sem=send, recv_sem=recv, device_id=dev, device_id_type=MESH
    )


def greet(peers):
    barrier = pltpu.get_barrier_semaphore()
    for peer in peers:
        pl.semaphore_signal(barrier, inc=1, device_id=peer, device_id_type=MESH)
    pl.semaphore_wait(barrier, len(peers))


def gather_kernel(spread, *refs):
    count = len(spread)
    small_in, ins = refs[0], refs[1 : 1 + count]
    small_out, outs = refs[1 + count], refs[2 + count : 2 + 2 * count]
    sends, recvs = refs[2 + 2 * count :]
    d, x = lax.axis_index("dp"), lax.axis_index("mp")
    core, yy, zz = d % 2, (d // 2) % 2, (d // 4) % 2
    to_x = (d, 1 - x)
    to_core = (d + 1 - 2 * core, x)
    to_y = (d + 2 - 4 * yy, x)
    to_z = (d + 4 - 8 * zz, x)
    greet([to_x, to_core, to_y, to_z])
    units = [(layer, t) for layer in range(2) for t in range(count)]

    def part(ref, layer, start, size):
        return ref.at[layer, pl.ds(pl.multiple_of(start, 16), size)]

    def hop(u, stage):
        layer, t = units[u]
        rows = ins[t].shape[1]
        piece = rows // (8 if spread[t] else 4)
        base = core * (rows // 2)
        src = outs[t]
        if stage == 0:
            start = base + (zz * 2 + yy if spread[t] else yy) * piece
            size, dev, src = piece, to_x, ins[t]
        elif stage == 1:
            start = base + (zz * 2 + yy if spread[t] else yy) * piece
            size, dev = piece, to_y
        elif stage == 2:
            start, size, dev = base + zz * 2 * piece, 2 * piece, to_z
        else:
            start, size, dev = base, rows // 2, to_core
        return rdma(
            part(src, layer, start, size),
            part(outs[t], layer, start, size),
            sends.at[u, stage],
            recvs.at[u, stage],
            dev,
        )

    total = len(units)
    extra = rdma(small_in, small_out, sends.at[total, 0], recvs.at[total, 0], to_x)
    extra.start()
    for u in range(total):
        hop(u, 0).start()
    for step in range(total + 3):
        u = step - 2
        if 0 <= u < total:
            if spread[units[u][1]]:
                hop(u, 2).wait_recv()
            else:
                hop(u, 1).wait_recv()
            hop(u, 3).start()
        u = step - 1
        if 0 <= u < total and spread[units[u][1]]:
            hop(u, 1).wait_recv()
            hop(u, 2).start()
        u = step
        if u < total:
            hop(u, 0).wait_recv()
            hop(u, 1).start()
    extra.wait()
    for u in range(total):
        hop(u, 3).wait_recv()
        for stage in range(4):
            if stage != 2 or spread[units[u][1]]:
                hop(u, stage).wait_send()


def gather_weights(small, tensors, spread):
    count = len(tensors)
    any_spec = pl.BlockSpec(memory_space=pltpu.HBM)
    return pl.pallas_call(
        functools.partial(gather_kernel, spread),
        out_shape=[jax.ShapeDtypeStruct(a.shape, a.dtype) for a in (small, *tensors)],
        in_specs=[any_spec] * (1 + count),
        out_specs=[any_spec] * (1 + count),
        scratch_shapes=[
            pltpu.SemaphoreType.DMA((2 * count + 1, 4)),
            pltpu.SemaphoreType.DMA((2 * count + 1, 4)),
        ],
        compiler_params=pltpu.CompilerParams(collective_id=0, has_side_effects=True),
        name="gather_weights",
    )(small, *tensors)


def chunks_of(rows, dp):
    unit = 16 * dp
    units, out, at = rows // unit, [], 0
    while units > 0:
        size = 3 if units > 6 else (2 if units > 3 else 1)
        size = min(size, units)
        out.append((at, size * unit))
        at += size * unit
        units -= size
    return out


def reduce_kernel(dp, chunks, g, out, loc, cbuf, xbuf, ybuf, zbuf, cs, cr, xs, xr, ys, yr, zs, zr, bs, br, as_, ar, es, er, ls, os):
    Z = 4
    Y = dp // (2 * Z)
    d, x = lax.axis_index("dp"), lax.axis_index("mp")
    core, yy, zz = d % 2, (d // 2) % Y, d // (2 * Y)
    to_x = (d, 1 - x)
    to_core = (d + 1 - 2 * core, x)
    ys_peer = [(yy + i) % Y for i in range(1, Y)]
    zs_peer = [(zz + i) % Z for i in range(1, Z)]
    to_y = [((zz * Y + p) * 2 + core, x) for p in ys_peer]
    to_z = [((p * Y + yy) * 2 + core, x) for p in zs_peer]
    greet([to_core, to_x] + to_y + to_z)
    K = len(chunks)

    def al(v):
        return pl.multiple_of(v, 16)

    def sizes(k):
        at, rows = chunks[k]
        return at, rows, rows // 2, rows // 2 // Y, rows // 2 // Y // Z

    def core_copy(k):
        at, rows, half, _, _ = sizes(k)
        return rdma(
            g.at[:, pl.ds(al(at + (1 - core) * half), half)],
            cbuf.at[:, pl.ds(at // 2, half)],
            cs.at[k], cr.at[k], to_core,
        )

    def load(k):
        at, rows, half, _, _ = sizes(k)
        return pltpu.make_async_copy(
            g.at[:, pl.ds(al(at + core * half), half)], loc.at[k % 2, :, pl.ds(0, half)], ls.at[k % 2]
        )

    def x_copy(k):
        at, rows, half, _, _ = sizes(k)
        return rdma(cbuf.at[1, pl.ds(at // 2, half)], xbuf.at[pl.ds(at // 2, half)], xs.at[k], xr.at[k], to_x)

    def y_copy(k, i):
        at, rows, half, quarter, _ = sizes(k)
        base = at // (2 * Y) * (Y - 1)
        return rdma(
            cbuf.at[0, pl.ds(al(at // 2 + ys_peer[i] * quarter), quarter)],
            ybuf.at[pl.ds(base + i * quarter, quarter)],
            ys.at[k, i], yr.at[k, i], to_y[i],
        )

    def z_copy(k, i):
        at, rows, half, quarter, piece = sizes(k)
        base = at // (2 * Y * Z) * (Z - 1)
        return rdma(
            cbuf.at[0, pl.ds(al(at // 2 + yy * quarter + zs_peer[i] * piece), piece)],
            zbuf.at[pl.ds(base + i * piece, piece)],
            zs.at[k, i], zr.at[k, i], to_z[i],
        )

    def mine(k):
        at, rows, half, quarter, piece = sizes(k)
        return (
            pl.ds(al(at // 2 + yy * quarter + zz * piece), piece),
            pl.ds(al(at + core * half + yy * quarter + zz * piece), piece),
        )

    def own_copy(k):
        a, b = mine(k)
        return pltpu.make_async_copy(cbuf.at[0, a], out.at[b], os.at[k])

    def zb_copy(k, i):
        a, b = mine(k)
        return rdma(cbuf.at[0, a], out.at[b], bs.at[k, i], br.at[k, i], to_z[i])

    def yb_copy(k, i):
        at, rows, half, quarter, piece = sizes(k)
        rows_ = pl.ds(al(at + core * half + yy * quarter), quarter)
        return rdma(out.at[rows_], out.at[rows_], as_.at[k, i], ar.at[k, i], to_y[i])

    def cb_copy(k):
        at, rows, half, quarter, piece = sizes(k)
        rows_ = pl.ds(al(at + core * half), half)
        return rdma(out.at[rows_], out.at[rows_], es.at[k], er.at[k], to_core)

    f32, bf = jnp.float32, jnp.bfloat16

    def s1(k):
        at, rows, half, quarter, piece = sizes(k)
        if k + 1 < K:
            load(k + 1).start()
        load(k).wait()
        core_copy(k).wait_recv()
        for m in (1, 0):
            r = cbuf.at[m, pl.ds(at // 2, half)]
            r[...] = (r[...].astype(f32) + loc[k % 2, m, :half].astype(f32)).astype(bf)
            if m == 1:
                x_copy(k).start()

    def s2(k):
        at, rows, half, quarter, piece = sizes(k)
        x_copy(k).wait_recv()
        r = cbuf.at[0, pl.ds(at // 2, half)]
        r[...] = (r[...].astype(f32) + xbuf[at // 2 : at // 2 + half].astype(f32)).astype(bf)
        for i in range(Y - 1):
            y_copy(k, i).start()

    def s3(k):
        at, rows, half, quarter, piece = sizes(k)
        base = at // (2 * Y) * (Y - 1)
        r = cbuf.at[0, pl.ds(al(at // 2 + yy * quarter), quarter)]
        acc = r[...].astype(f32)
        for i in range(Y - 1):
            y_copy(k, i).wait_recv()
            acc = acc + ybuf[base + i * quarter : base + (i + 1) * quarter].astype(f32)
        r[...] = acc.astype(bf)
        for i in range(Z - 1):
            z_copy(k, i).start()

    def s4(k):
        at, rows, half, quarter, piece = sizes(k)
        base = at // (2 * Y * Z) * (Z - 1)
        a, b = mine(k)
        r = cbuf.at[0, a]
        acc = r[...].astype(f32)
        for i in range(Z - 1):
            z_copy(k, i).wait_recv()
            acc = acc + zbuf[base + i * piece : base + (i + 1) * piece].astype(f32)
        r[...] = acc.astype(bf)
        own_copy(k).start()
        for i in range(Z - 1):
            zb_copy(k, i).start()

    def s5(k):
        own_copy(k).wait()
        for i in range(Z - 1):
            zb_copy(k, i).wait_recv()
        for i in range(Y - 1):
            yb_copy(k, i).start()

    def s6(k):
        for i in range(Y - 1):
            yb_copy(k, i).wait_recv()
        cb_copy(k).start()

    for k in range(K):
        core_copy(k).start()
    load(0).start()
    stages = [s1, s2, s3, s4, s5, s6]
    lag = [0, 4, 5, 6, 7, 8]
    for t in range(K + lag[-1]):
        for stage, off in reversed(list(zip(stages, lag))):
            if 0 <= t - off < K:
                stage(t - off)
    for k in range(K):
        cb_copy(k).wait_recv()
        core_copy(k).wait_send()
        x_copy(k).wait_send()
        cb_copy(k).wait_send()
        for i in range(Y - 1):
            y_copy(k, i).wait_send()
            yb_copy(k, i).wait_send()
        for i in range(Z - 1):
            z_copy(k, i).wait_send()
            zb_copy(k, i).wait_send()


def reduce_gradients(dp, packed):
    rows = packed.shape[1]
    chunks = chunks_of(rows, dp)
    K = len(chunks)
    Z = 4
    Y = dp // (2 * Z)
    biggest = max(size for _, size in chunks) // 2
    hbm = pl.BlockSpec(memory_space=pltpu.HBM)
    bf = jnp.bfloat16
    dma = pltpu.SemaphoreType.DMA
    return pl.pallas_call(
        functools.partial(reduce_kernel, dp, chunks),
        out_shape=jax.ShapeDtypeStruct((rows, W), bf),
        in_specs=[hbm],
        out_specs=hbm,
        scratch_shapes=[
            pltpu.VMEM((2, 2, biggest, W), bf),
            pltpu.VMEM((2, rows // 2, W), bf),
            pltpu.VMEM((rows // 2, W), bf),
            pltpu.VMEM((rows // (2 * Y) * (Y - 1), W), bf),
            pltpu.VMEM((rows // (2 * Y * Z) * (Z - 1), W), bf),
            dma((K,)), dma((K,)), dma((K,)), dma((K,)),
            dma((K, Y - 1)), dma((K, Y - 1)),
            dma((K, Z - 1)), dma((K, Z - 1)),
            dma((K, Z - 1)), dma((K, Z - 1)),
            dma((K, Y - 1)), dma((K, Y - 1)),
            dma((K,)), dma((K,)), dma((2,)), dma((K,)),
        ],
        compiler_params=pltpu.CompilerParams(
            collective_id=1, has_side_effects=True, vmem_limit_bytes=56 * 2**20
        ),
        name="reduce_gradients",
    )(packed)


def layer_norm(values, scaling, shifting):
    average = jnp.mean(values, axis=-1, keepdims=True)
    centred = values - average
    spread = jnp.mean(centred * centred, axis=-1, keepdims=True)
    return centred * lax.rsqrt(spread + 1e-05) * scaling + shifting


def positions(lengths_row, row_count, head_size):
    finish = jnp.cumsum(lengths_row, dtype=jnp.int32)
    counter = jnp.arange(row_count, dtype=jnp.int32)
    passed = counter[:, None] >= finish[None, :]
    segment = jnp.sum(passed.astype(jnp.int32), axis=1, dtype=jnp.int32)
    start_at = jnp.sum(jnp.where(passed, lengths_row[None, :], 0), axis=1, dtype=jnp.int32)
    offset = (counter - start_at).astype(jnp.float32)
    half_size = head_size // 2
    frequency = jnp.exp(
        jnp.arange(half_size, dtype=jnp.float32) * (-2.0 * math.log(10000.0) / head_size)
    )
    angles = offset[:, None] * frequency[None, :]
    same_mol = (segment[:, None] == segment[None, :]).astype(jnp.float32)
    return (jnp.cos(angles)[:, None, :], jnp.sin(angles)[:, None, :], same_mol)


def rotate(vectors, cosines, sines):
    half_size = vectors.shape[-1] // 2
    leading = vectors[..., :half_size]
    trailing = vectors[..., half_size:]
    return jnp.concatenate(
        [leading * cosines - trailing * sines, trailing * cosines + leading * sines], axis=-1
    )


def features(vectors, random_proj):
    scaled = vectors * vectors.shape[-1] ** (-0.25)
    return jax.nn.softplus(
        jnp.einsum("thd,hdm->thm", scaled, random_proj, precision=lax.Precision.HIGH)
    )


def attend(queries, key_rows, values, random_proj, cosines, sines, same_mol):
    row_count, model_width = queries.shape
    head_count, head_size = (random_proj.shape[0], random_proj.shape[1])
    shaped = (row_count, head_count, head_size)
    query_feats = features(rotate(queries.reshape(shaped), cosines, sines), random_proj)
    key_feats = features(rotate(key_rows.reshape(shaped), cosines, sines), random_proj)
    scores = jnp.einsum("thm,shm->hts", query_feats, key_feats) * same_mol[None]
    numerator = jnp.einsum("hts,shd->thd", scores, values.reshape(shaped))
    denominator = jnp.sum(scores, axis=2).T[:, :, None]
    return (numerator / denominator).reshape(row_count, model_width)


def gelu_exact(values):
    return jax.nn.gelu(values, approximate=False)


def on_device(
    dp,
    tokens,
    cotangent,
    lengths,
    random_proj,
    attn_weight,
    attn_bias,
    out_weight,
    norm_gains,
    biases,
    up_weight,
    up_bias,
    down_weight,
):
    f32, bf = jnp.float32, jnp.bfloat16
    layers = attn_weight.shape[0]
    model = tokens.shape[1]
    part = attn_weight.shape[3]
    hidden_part = up_weight.shape[2]
    blocks = hidden_part // part
    x = lax.axis_index("mp")
    heads = random_proj.shape[1] // 2
    small = jnp.concatenate(
        [
            attn_bias.reshape(-1, part),
            up_bias.reshape(-1, part),
            jnp.zeros((16 - layers * (3 + blocks), part), bf),
        ]
    )
    gathered = gather_weights(
        small,
        (attn_weight.reshape(layers, -1, part), out_weight, up_weight, down_weight),
        (True, True, False, True),
    )
    other_attn_bias = gathered[0][: 3 * layers].reshape(layers, 3, part)
    other_up_bias = gathered[0][3 * layers : (3 + blocks) * layers].reshape(layers, hidden_part)
    other_attn = gathered[1].reshape(attn_weight.shape)
    attn_b = jnp.concatenate([attn_bias, other_attn_bias], axis=2).astype(f32)
    up_b = jnp.concatenate([up_bias, other_up_bias], axis=1).astype(f32)
    attn_w = jnp.concatenate([attn_weight, other_attn], axis=3)
    out_w = jnp.concatenate([out_weight, gathered[2]], axis=1)
    up_w = jnp.concatenate([up_weight, gathered[3]], axis=2)
    down_w = jnp.concatenate([down_weight, gathered[4]], axis=1)
    proj = jnp.where(x == 0, random_proj, jnp.roll(random_proj, heads, axis=1))
    gain_values = norm_gains.astype(f32)
    shift_values = biases.astype(f32)
    cosines, sines, same_mol = positions(lengths[0], tokens.shape[0], random_proj.shape[2])
    current = tokens.astype(f32)
    kept = []
    for layer in range(layers):
        normed = layer_norm(current, gain_values[layer, 0], shift_values[layer, 0]).astype(bf)
        projected = [
            jnp.dot(normed, attn_w[layer, j], preferred_element_type=f32) + attn_b[layer, j]
            for j in range(3)
        ]
        context = attend(*projected, proj[layer], cosines, sines, same_mol).astype(bf)
        middle = (
            current
            + jnp.dot(context, out_w[layer], preferred_element_type=f32)
            + shift_values[layer, 1]
        )
        second = layer_norm(middle, gain_values[layer, 1], shift_values[layer, 2]).astype(bf)
        hidden = jnp.dot(second, up_w[layer], preferred_element_type=f32) + up_b[layer]
        active = gelu_exact(hidden).astype(bf)
        kept.append((current, normed, projected, context, middle, second, hidden, active))
        current = (
            middle
            + jnp.dot(active, down_w[layer], preferred_element_type=f32)
            + shift_values[layer, 3]
        )
    stack_out = current.astype(bf)
    grad_now = cotangent.astype(f32)
    rows = []
    smalls = []

    def halves(grad, axis):
        return jnp.split(grad.astype(bf), 2, axis=axis)

    for layer in reversed(range(layers)):
        layer_in, normed, projected, context, middle, second, hidden, active = kept[layer]
        branch_grad = grad_now.astype(bf)
        down_grad = jnp.dot(active.T, branch_grad, preferred_element_type=f32).astype(bf)
        active_grad = jnp.dot(branch_grad, down_w[layer].T, preferred_element_type=f32)
        hidden_grad = jax.vjp(gelu_exact, hidden)[1](active_grad)[0].astype(bf)
        up_grad = jnp.dot(second.T, hidden_grad, preferred_element_type=f32).astype(bf)
        up_shift_grad = jnp.sum(hidden_grad.astype(f32), axis=0)
        second_grad = jnp.dot(hidden_grad, up_w[layer].T, preferred_element_type=f32)
        middle_grad, gain_two, shift_two = jax.vjp(
            layer_norm, middle, gain_values[layer, 1], shift_values[layer, 2]
        )[1](second_grad)
        middle_grad = middle_grad + grad_now
        attn_grad = middle_grad.astype(bf)
        out_grad = jnp.dot(context.T, attn_grad, preferred_element_type=f32).astype(bf)
        context_grad = jnp.dot(attn_grad, out_w[layer].T, preferred_element_type=f32)

        def attend_local(queries, key_rows, values):
            return attend(queries, key_rows, values, proj[layer], cosines, sines, same_mol)

        triple = [g.astype(bf) for g in jax.vjp(attend_local, *projected)[1](context_grad)]
        attn_grads = [
            jnp.dot(normed.T, g, preferred_element_type=f32).astype(bf) for g in triple
        ]
        attn_bias_grad = jnp.stack([jnp.sum(g.astype(f32), axis=0) for g in triple])
        normed_grad = sum(
            jnp.dot(triple[j], attn_w[layer, j].T, preferred_element_type=f32) for j in range(3)
        )
        input_grad, gain_one, shift_one = jax.vjp(
            layer_norm, layer_in, gain_values[layer, 0], shift_values[layer, 0]
        )[1](normed_grad)
        full_rows = jnp.stack(
            [
                gain_one,
                gain_two,
                shift_one,
                jnp.sum(attn_grad.astype(f32), axis=0),
                shift_two,
                jnp.sum(branch_grad.astype(f32), axis=0),
            ]
        ).reshape(6, 2, part)
        full_rows = jnp.where(x == 0, full_rows, full_rows[:, ::-1])
        small_rows = jnp.concatenate(
            [
                full_rows,
                attn_bias_grad.reshape(3, 2, part),
                up_shift_grad.reshape(2, blocks, part).swapaxes(0, 1),
            ]
        ).swapaxes(0, 1)
        smalls.append(small_rows.astype(bf))
        grad_now = input_grad + middle_grad
        rows.append(
            [
                jnp.stack(
                    [jnp.concatenate([a[:, i * part : (i + 1) * part] for i in range(2)]) for a in halves(down_grad, 0)]
                ),
                jnp.stack(
                    [jnp.concatenate([a[:, i * part : (i + 1) * part] for i in range(blocks)]) for a in halves(up_grad, 1)]
                ),
                jnp.stack(
                    [jnp.concatenate([a[:, i * part : (i + 1) * part] for i in range(2)]) for a in halves(out_grad, 0)]
                ),
                jnp.stack(
                    [jnp.concatenate([a[:, i * part : (i + 1) * part] for a in attn_grads]) for i in range(2)]
                ),
            ]
        )
    small_rows = jnp.concatenate(smalls, axis=1)
    pad = 16 * dp - small_rows.shape[1]
    small_rows = jnp.pad(small_rows, ((0, 0), (0, pad), (0, 0)))
    packed = jnp.concatenate(rows[0] + rows[1] + [small_rows], axis=1)
    reduced = reduce_gradients(dp, packed)
    at = 0

    def take(count):
        nonlocal at
        block = reduced[at : at + count]
        at += count
        return block

    def columns(block, count):
        return jnp.concatenate(jnp.split(block, count), axis=1).astype(f32)

    found = [None] * layers
    for layer in reversed(range(layers)):
        down_g = columns(take(2 * hidden_part), 2)
        up_g = columns(take(blocks * model), blocks)
        out_g = columns(take(2 * part), 2)
        attn_g = take(3 * model).reshape(3, model, part).astype(f32)
        found[layer] = [attn_g, out_g, up_g, down_g]
    small_g = []
    for _ in range(layers):
        small_g.append(take(9 + blocks).astype(f32))
    small_g = jnp.stack(small_g[::-1])
    big = [jnp.stack([found[layer][i] for layer in range(layers)]) for i in range(4)]
    return (
        stack_out,
        grad_now,
        big[0],
        small_g[:, 6:9],
        big[1],
        small_g[:, :2],
        small_g[:, 2:6],
        big[2],
        small_g[:, 9 : 9 + blocks].reshape(layers, hidden_part),
        big[3],
    )


def solution(mesh):
    return jax.shard_map(
        functools.partial(on_device, mesh.shape["dp"]),
        mesh=mesh,
        in_specs=(
            P(("dp", "mp"), None),
            P(("dp", "mp"), None),
            P(("dp", "mp"), None),
            P(),
            P(None, None, None, "mp"),
            P(None, None, "mp"),
            P(None, "mp", None),
            P(),
            P(),
            P(None, None, "mp"),
            P(None, "mp"),
            P(None, "mp", None),
        ),
        out_specs=(
            P(("dp", "mp"), None),
            P(("dp", "mp"), None),
            P(None, None, None, "mp"),
            P(None, None, "mp"),
            P(None, "mp", None),
            P(None, None, "mp"),
            P(None, None, "mp"),
            P(None, None, "mp"),
            P(None, "mp"),
            P(None, "mp", None),
        ),
        check_vma=False,
    )
```

time: 1010 us -> 521 us (0.52)
  waiting for transfers between devices: 540 us -> 0 us
  Pallas kernels: 0 us -> 314 us
  blocking collectives: 167 us -> 0 us
  matrix products: 168 us -> 91.5 us
  other arithmetic: 74.8 us -> 58.8 us
  between operations: 16 us -> 2.8 us
  local copies, waits for them, and re-layouts: 33.8 us -> 43.9 us
    psum x1 -> x0, waiting for transfers between devices: 432 us -> none  [on_device(): lax.psum((shares[0], shares[1], shares[2], shares[3], shares[4], shares[5...]
    pallas_call x0 -> x2, Pallas kernels: none -> 314 us  [the longest x1 218 us: reduce_gradients(): pl.pallas_call(functools.partial(reduce_kernel, dp, chunks), out_shape=ja...]
    reduce_scatter x10 -> x0, waiting for transfers between devices: 108 us -> none  [the longest x2 33.9 us: on_device(): lax.psum_scatter(jnp.dot(active, down_full, preferred_element_type=jnp.fl...]
    all_gather x9 -> x0, blocking collectives: 102 us -> none  [the longest x2 26.9 us: on_device(): rows_grad = lax.all_gather(branch_grad, 'mp', axis=0, tiled=True)]
    dot_general x44 -> x56, matrix products: 168 us -> 91.5 us  [the longest x2 21.8 us: on_device(): jnp.dot(second, up_w[layer], preferred_element_type=f32) + up_b[layer]]
    psum x1 -> x0, blocking collectives: 64.7 us -> none  [on_device(): lax.psum((shares[0], shares[1], shares[2], shares[3], shares[4], shares[5...]
    unnamed x6 -> x13, other arithmetic: 0.01 us -> 18.5 us
    add x0 -> x6, local copies, waits for them, and re-layouts: none -> 13 us  [on_device(): jnp.dot(normed, attn_w[layer, j], preferred_element_type=f32)]
  transfers between devices with their start and end apart: 11 -> 0, of which waited for: 9 -> 0; matrix products, arithmetic and copies ran while one was open for 5% -> 0% of each run, Pallas kernels for 0% -> 0%
where the time goes in v1:
time: 521 us; the launch traced here: 511 us
  Pallas kernels  314 us (60%)
  matrix products  91.5 us (18%)
  other arithmetic  58.8 us (11%)
  local copies, waits for them, and re-layouts  43.9 us (8%)
    pallas_call x1, Pallas kernels, reduce_gradients(): pl.pallas_call(functools.partial(reduce_kernel, dp, chunks), out_shape=ja...  218 us
    pallas_call x1, Pallas kernels, gather_weights(): pl.pallas_call(functools.partial(gather_kernel, spread), out_shape=[jax.S...  96 us
    dot_general x2, matrix products, on_device(): jnp.dot(second, up_w[layer], preferred_element_type=f32) + up_b[layer]  21.8 us
    unnamed x248, local copies, waits for them, and re-layouts  19.3 us
    unnamed x13, other arithmetic  18.5 us
    another operation x4, other arithmetic, on_device(): jnp.stack([found[layer][i] for layer in range(layers)])  13.9 us
    add x6, local copies, waits for them, and re-layouts, on_device(): jnp.dot(normed, attn_w[layer, j], preferred_element_type=f32)  13 us

profile of v1, /device:TPU:0, one launch (start us, length us, event | category | flops | bytes accessed | tf_op | source)
XLA Modules:
  0.0 510.6 jit_solution(3969495107727923021)
XLA Ops:
  5.9 96.0 %gather_weights.1 = (bf16[16,384]{1,0:T(8,128)(2,1)}, bf16[2,2304,384]{2,1,0:T(8,128)(2,1)}, bf16[2,384,768]{2,1,0:T(8,128)(2,1)}, bf16[2,768,1536]{2,1,0:T(8,128)(2,1)}, bf16[2,1536,768]{2,1,0:T(8,128)(2,1)}) custom-call(bf16[16,384]{1,0:T(8,128)(2,1)} %maximum_maximum_fusion.refs_0_, bf16[2,2304,384]{2,1,0:T(8,128)(2,1)} %bitcast.338, ...), custom_call_target="tpu_custom_call" | custom-call | tf_op jit(solution)/shard_map/gather_weights/pallas_call | solution.py:101
  102.0 4.8 fusion.96
  108.7 1.4 convolution_add_fusion.9
  110.1 2.3 copy.71
  112.6 1.4 convolution_add_fusion.10
  114.1 2.3 copy.70
  116.4 1.7 multiply_subtract_fusion.2
  121.6 1.9 copy.69
  123.5 2.4 divide_convert_fusion.1
  127.1 1.7 fusion.207
  129.5 3.1 constant_dynamic-update-slice_fusion.3
  134.6 10.2 %multiply_convert_fusion.1 = (bf16[256,3072]{1,0:T(8,128)(2,1)S(1)}, f32[256,3072]{1,0:T(8,128)}, f32[256,3072]{1,0:T(8,128)}) fusion(f32[3072]{0:T(1024)S(1)} %bitcast.382, bf16[2,768,3072]{2,1,0:T(8,128)(2,1)S(1)} %constant_dynamic-update-slice_fusion.2, f32[256,768]{1,0:T(8,128)S(1)} %copy-done.19, f32[768]{0:T(1024)S(1)} %get-tuple-element.84, ...), kind=kOutput, calls=%fused_computation.59 | convolution fusion | flops 1260847104 | bytes 13391872 | tf_op jit(solution)/shard_map/dot_general | solution.py:444
  145.2 2.4 slice-done.2
  148.1 1.5 fusion.208
  149.5 2.2 copy-done.36
  153.3 1.4 convolution_add_fusion.5
  154.6 2.3 copy.75
  156.9 2.6 convolution_add_fusion.6
  159.6 2.3 copy.74
  161.9 1.7 multiply_subtract_fusion
  164.4 3.1 multiply_reduce_fusion
  168.7 1.9 copy.73
  170.7 2.5 divide_convert_fusion
  174.6 11.7 %multiply_convert_fusion = (bf16[256,3072]{1,0:T(8,128)(2,1)S(1)}, f32[256,3072]{1,0:T(8,128)S(1)}, f32[256,3072]{1,0:T(8,128)}) fusion(f32[3072]{0:T(1024)S(1)} %bitcast.381, bf16[2,768,3072]{2,1,0:T(8,128)(2,1)} %copy-done.37, f32[256,768]{1,0:T(8,128)S(1)} %get-tuple-element.242, f32[768]{0:T(1024)S(1)} %copy-done.60, f32[768]{0:T(1024)S(1)} %copy-done.57, ...), kind=kOutput, calls=%fused_computation.46 | convolution fusion | flops 1260847104 | bytes 13389824 | tf_op jit(solution)/shard_map/dot_general | solution.py:444
  186.4 2.1 fusion.63
  189.5 4.4 fusion.211
  193.9 4.5 multiply_reduce_fusion.3
  207.3 1.3 bitcast_reduce_fusion.1
  208.6 1.3 multiply_reduce_fusion.4
  211.2 5.1 %fusion.210 = (bf16[3072]{0:T(1024)(128)(2,1)}, bf16[256,3072]{1,0:T(8,128)(2,1)S(1)}) fusion(f32[256,3072]{1,0:T(8,128)} %get-tuple-element.122, f32[256,3072]{1,0:T(8,128)} %get-tuple-element.234, bf16[2,3072,768]{2,1,0:T(8,128)(2,1)S(1)} %bitcast.365, f32[256,768]{1,0:T(8,128)S(1)} %get-tuple-element.110), kind=kOutput, calls=%fused_computation.445 | convolution fusion | flops 1219949568 | bytes 13375488 | tf_op jit(solution)/shard_map/dot_general | solution.py:464
  216.4 4.6 multiply_reduce_fusion.2
  233.1 1.4 convolution_convert_fusion.3
  235.5 2.8 maximum_dynamic-update-slice_fusion.3
  238.4 2.0 convolution_convert_fusion.2
  241.7 2.8 maximum_dynamic-update-slice_fusion.2
  248.7 2.3 maximum_dynamic-update-slice_fusion.5
  251.1 1.5 convolution_convert_fusion.1
  253.5 2.7 maximum_dynamic-update-slice_fusion.1
  256.2 1.6 convolution_convert_fusion
  258.8 2.6 maximum_dynamic-update-slice_fusion
  266.5 2.3 maximum_dynamic-update-slice_fusion.4
  270.7 217.5 %reduce_gradients.1 = bf16[18688,384]{1,0:T(8,128)(2,1)} custom-call(bf16[2,18688,384]{2,1,0:T(8,128)(2,1)} %fusion.118.g), custom_call_target="tpu_custom_call" | custom-call | tf_op jit(solution)/shard_map/reduce_gradients/pallas_call | solution.py:301
  488.3 2.5 fusion.191
  490.8 4.1 maximum_convert_fusion.2
  494.8 2.1 copy-done
  497.7 1.6 maximum_convert_fusion.3
  501.0 4.2 maximum_convert_fusion
  506.3 4.1 maximum_convert_fusion.1
  (411 shorter events, 61.4 us)
Async XLA Ops:
  2.0 118.3 %copy-start.104 = (f32[768]{0:T(1024)}, f32[768]{0:T(1024)S(1)}, u32[]{:S(2)}) copy-start(f32[768]{0:T(1024)S(1)} %get-tuple-element.86) | copy-start | bytes 9220
  2.0 132.6 %copy-start.58 = (f32[768]{0:T(1024)}, f32[768]{0:T(1024)S(1)}, u32[]{:S(2)}) copy-start(f32[768]{0:T(1024)S(1)} %get-tuple-element.84) | copy-start | bytes 9220
  3.7 119.9 %copy-start.4 = (f32[256,256]{0,1:T(8,128)}, f32[256,256]{0,1:T(8,128)S(1)}, u32[]{:S(2)}) copy-start(f32[256,256]{0,1:T(8,128)S(1)} %compare_convert_fusion) | copy-start | bytes 786436
  101.9 4.9 copy-start.85
  101.9 5.7 %copy-start.103 = (bf16[2,2,768]{2,1,0:T(2,128)(2,1)S(1)}, bf16[2,2,768]{2,1,0:T(2,128)(2,1)}, u32[]{:S(2)}) copy-start(bf16[2,2,768]{2,1,0:T(2,128)(2,1)} %param.20) | copy-start | bytes 18436
  102.0 6.3 %copy-start.10 = (bf16[256,768]{1,0:T(8,128)(2,1)S(1)}, bf16[256,768]{1,0:T(8,128)(2,1)}, u32[]{:S(2)}) copy-start(bf16[256,768]{1,0:T(8,128)(2,1)} %param.13) | copy-start | bytes 1179652
  106.8 7.3 %copy-start.25 = (bf16[768,768]{1,0:T(8,128)(2,1)}, bf16[768,768]{1,0:T(8,128)(2,1)S(1)}, u32[]{:S(2)}) copy-start(bf16[768,768]{1,0:T(8,128)(2,1)S(1)} %get-tuple-element.146) | copy-start | bytes 3538948
  106.8 7.3 %copy-start.27 = (bf16[768,768]{1,0:T(8,128)(2,1)}, bf16[768,768]{1,0:T(8,128)(2,1)S(1)}, u32[]{:S(2)}) copy-start(bf16[768,768]{1,0:T(8,128)(2,1)S(1)} %get-tuple-element.145) | copy-start | bytes 3538948
  108.2 12.0 %copy-start.61 = (f32[768]{0:T(1024)}, f32[768]{0:T(1024)S(1)}, u32[]{:S(2)}) copy-start(f32[768]{0:T(1024)S(1)} %get-tuple-element.90) | copy-start | bytes 9220
  108.2 26.3 %copy-start.55 = (f32[768]{0:T(1024)}, f32[768]{0:T(1024)S(1)}, u32[]{:S(2)}) copy-start(f32[768]{0:T(1024)S(1)} %get-tuple-element.89) | copy-start | bytes 9220
  108.4 11.9 %copy-start.65 = (f32[256]{0:T(256)}, f32[256]{0:T(256)S(1)}, u32[]{:S(2)}) copy-start(f32[256]{0:T(256)S(1)} %broadcast_multiply_fusion.3) | copy-start | bytes 3076
  108.6 3.8 copy-start.87
  108.7 11.6 %copy-start.93 = (f32[256]{0:T(256)}, f32[256]{0:T(256)S(1)}, u32[]{:S(2)}) copy-start(f32[256]{0:T(256)S(1)} %fusion.150) | copy-start | bytes 3076
  112.6 5.4 %copy-start.50 = (f32[256,32]{0,1:T(8,128)}, f32[256,32]{0,1:T(8,128)S(1)}, u32[]{:S(2)}) copy-start(f32[256,32]{0,1:T(8,128)S(1)} %get-tuple-element.226) | copy-start | bytes 98308
  112.6 5.4 %copy-start.52 = (f32[256,32]{0,1:T(8,128)}, f32[256,32]{0,1:T(8,128)S(1)}, u32[]{:S(2)}) copy-start(f32[256,32]{0,1:T(8,128)S(1)} %get-tuple-element.227) | copy-start | bytes 98308
  112.6 5.4 %copy-start.46 = (f32[2,12,64,32]{2,3,1,0:T(8,128)S(1)}, f32[2,12,64,32]{2,3,1,0:T(8,128)}, u32[]{:S(2)}) copy-start(f32[2,12,64,32]{2,3,1,0:T(8,128)} %param.16) | copy-start | bytes 589828
  129.5 3.6 slice-start.4
  129.5 3.7 slice-start.5
  133.2 11.7 %slice-start = ((s8[4718592]{0:T(1024)(128)(4,1)}), s8[4194304]{0:T(1024)(128)(4,1)S(1)}, s32[]{:S(2)}) async-start(s8[4718592]{0:T(1024)(128)(4,1)} %bitcast.336), calls=%async_computation | async-start | bytes 8388608
  133.9 10.9 %copy-start.37 = (bf16[2,768,3072]{2,1,0:T(8,128)(2,1)}, bf16[2,768,3072]{2,1,0:T(8,128)(2,1)S(1)}, u32[]{:S(2)}) copy-start(bf16[2,768,3072]{2,1,0:T(8,128)(2,1)S(1)} %constant_dynamic-update-slice_fusion.2) | copy-start | bytes 28311556
  134.3 10.5 %copy-start.69 = (f32[256]{0:T(256)}, f32[256]{0:T(256)S(1)}, u32[]{:S(2)}) copy-start(f32[256]{0:T(256)S(1)} %broadcast_multiply_fusion.2) | copy-start | bytes 3076
  134.5 10.3 %copy-start.89 = (f32[256]{0:T(256)}, f32[256]{0:T(256)S(1)}, u32[]{:S(2)}) copy-start(f32[256]{0:T(256)S(1)} %multiply_reduce_fusion.12) | copy-start | bytes 3076
  134.6 10.2 %copy-start.83 = (f32[256]{0:T(256)}, f32[256]{0:T(256)S(1)}, u32[]{:S(2)}) copy-start(f32[256]{0:T(256)S(1)} %fusion.151) | copy-start | bytes 3076
  134.6 10.3 %slice-start.1 = ((s8[4718592]{0:T(1024)(128)(4,1)}), s8[524288]{0:T(1024)(128)(4,1)S(1)}, s32[]{:S(2)}) async-start(s8[4718592]{0:T(1024)(128)(4,1)} %bitcast.336), calls=%async_computation.1 | async-start | bytes 1048576
  144.8 3.2 copy-start.32
  148.0 3.7 copy-start.36
  148.0 4.6 copy-start.63
  148.0 4.6 copy-start.73
  148.0 5.2 %copy-start.7 = (bf16[768,768]{1,0:T(8,128)(2,1)S(1)}, bf16[768,768]{1,0:T(8,128)(2,1)}, u32[]{:S(2)}) copy-start(bf16[768,768]{1,0:T(8,128)(2,1)} %get-tuple-element.143) | copy-start | bytes 3538948
  148.1 5.2 %copy-start.74 = (f32[768]{0:T(1024)S(1)}, f32[768]{0:T(1024)}, u32[]{:S(2)}) copy-start(f32[768]{0:T(1024)} %get-tuple-element.91) | copy-start | bytes 9220
  163.6 4.0 copy-start.29
  163.6 3.9 copy-start.107
  164.0 3.5 copy-start.42
  164.4 3.1 copy-start.44
  173.7 12.6 %slice-start.6 = ((s8[9437184]{0:T(1024)(128)(4,1)}), s8[4194304]{0:T(1024)(128)(4,1)S(1)}, s32[]{:S(2)}) async-start(s8[9437184]{0:T(1024)(128)(4,1)} %bitcast.364), calls=%async_computation.6 | async-start | bytes 8388608
  174.6 11.7 %slice-start.7 = ((s8[9437184]{0:T(1024)(128)(4,1)}), s8[4194304]{0:T(1024)(128)(4,1)S(1)}, s32[]{:S(2)}) async-start(s8[9437184]{0:T(1024)(128)(4,1)} %bitcast.364), calls=%async_computation.7 | async-start | bytes 8388608
  174.6 11.7 %slice-start.8 = ((s8[9437184]{0:T(1024)(128)(4,1)}), s8[1048576]{0:T(1024)(128)(4,1)S(1)}, s32[]{:S(2)}) async-start(s8[9437184]{0:T(1024)(128)(4,1)} %bitcast.364), calls=%async_computation.8 | async-start | bytes 2097152
  174.6 11.7 %copy-start.106 = (f32[768]{0:T(1024)S(1)}, f32[768]{0:T(1024)}, u32[]{:S(2)}) copy-start(f32[768]{0:T(1024)} %get-tuple-element.79) | copy-start | bytes 9220
  193.9 4.9 copy-start.54
  211.2 5.1 %copy-start.20 = (f32[256,768]{1,0:T(8,128)S(1)}, f32[256,768]{1,0:T(8,128)}, u32[]{:S(2)}) copy-start(f32[256,768]{1,0:T(8,128)} %get-tuple-element.233) | copy-start | bytes 2359300
  211.2 5.1 %copy-start.56 = (f32[768]{0:T(1024)S(1)}, f32[768]{0:T(1024)}, u32[]{:S(2)}) copy-start(f32[768]{0:T(1024)} %copy-done.55) | copy-start | bytes 9220
  211.2 5.1 %copy-start.70 = (f32[256]{0:T(256)S(1)}, f32[256]{0:T(256)}, u32[]{:S(2)}) copy-start(f32[256]{0:T(256)} %copy-done.69) | copy-start | bytes 3076
  211.2 5.1 %copy-start.84 = (f32[256]{0:T(256)S(1)}, f32[256]{0:T(256)}, u32[]{:S(2)}) copy-start(f32[256]{0:T(256)} %copy-done.83) | copy-start | bytes 3076
  216.4 4.6 copy-start.90
  266.5 3.1 copy-start.75
  266.5 3.2 copy-start.79
  266.5 3.3 copy-start.101
  488.3 8.7 %copy-start = (bf16[18688,384]{1,0:T(8,128)(2,1)S(1)}, bf16[18688,384]{1,0:T(8,128)(2,1)}, u32[]{:S(2)}) copy-start(bf16[18688,384]{1,0:T(8,128)(2,1)} %reduce_gradients.1) | copy-start | bytes 43057156
  (73 other events, 146.3 us)
